TPU v7x, 32 devices: a whole 2x2x4 slice. The times are simulated.
32 devices in a mesh: dom: 8 (over y, x, core), rep: 4 (over z).
Axes of the slice: x: 2, y: 2, z: 4, core: 2. Of those that a mesh axis runs over, the one named last changes fastest.
Arguments:
- features: float32 [2048, 256], P('dom'), may hold values from -6 to 6
- tile_values: bfloat16 [8, 64, 128, 128], P('dom', 'rep'), may hold values from 0 to 0.03125
- tile_rows: int32 [8, 64], P('dom', 'rep'), may hold values from 0 to 1
- tile_cols: int32 [8, 64], P('dom', 'rep'), may hold values from 0 to 15, as said below
- weight: float32 [256, 256], replicated, may hold values from -0.375 to 0.375
- bias: float32 [256], replicated, may hold values from -3 to 3
- cotangent: float32 [2048, 256], P('dom'), may hold values from -6 to 6
Outputs:
- activations: float32 [2048, 256], P('dom')
- grad_features: float32 [2048, 256], P('dom')
- grad_weight: float32 [256, 256], replicated
- grad_bias: float32 [256], replicated
Inputs may be any that keep to these rules, and one draw needn't show every extreme that they name: `tile_cols`: within each share of 16 consecutive tiles of a partition, every tile column 0 to 15 appears exactly once.
All inputs are finite; a program needn't handle non-finite values.
Results may differ from a plain program's by a relative error of at most 0.0003.
Values sent between devices are 32-bit elements; how exact they have to be, the bound alone decides.
A program may use at most 64 MiB of HBM per device.

v0:
```python
import jax
import jax.numpy as jnp
from jax import lax
from jax.sharding import PartitionSpec as P


def body(features, tile_values, tile_rows, tile_cols, weight, bias, cotangent):
    highest = lax.Precision.HIGHEST
    values = tile_values[0].astype(jnp.float32)
    row_ids = tile_rows[0]
    col_ids = tile_cols[0]
    tile_size = values.shape[1]
    node_rows = features.shape[0]
    feat_width = features.shape[1]
    row_blocks = node_rows // tile_size
    shard_piece = lax.all_gather(features, "dom", axis=0, tiled=True)
    block_count = shard_piece.shape[0] // tile_size
    blocks = shard_piece.reshape(block_count, tile_size, feat_width)
    offsets = col_ids[:, None]
    select = (offsets == jnp.arange(block_count, dtype=jnp.int32)[None, :]).astype(jnp.float32)
    selected = jnp.einsum("sn,nif->sif", select, blocks, precision=highest)
    products = jnp.einsum("sij,sjf->sif", values, selected, precision=highest)
    row_select = (row_ids[None, :] == jnp.arange(row_blocks, dtype=jnp.int32)[:, None]).astype(
        jnp.float32
    )
    partial_rows = jnp.einsum("bs,sif->bif", row_select, products, precision=highest).reshape(
        node_rows, feat_width
    )
    aggregated = lax.psum(partial_rows, "rep")
    before = jnp.dot(aggregated, weight, precision=highest) + bias
    gate_value = jax.nn.sigmoid(before)
    output = before * gate_value
    grad_pre = cotangent * gate_value * (1.0 + before * (1.0 - gate_value))
    messages = jnp.dot(grad_pre, weight.T, precision=highest)
    weight_term = jnp.dot(aggregated.T, grad_pre, precision=highest)
    activations, messages, weight_term, bias_term = (
        output,
        messages,
        weight_term,
        jnp.sum(grad_pre, axis=0),
    )
    grad_weight, grad_bias = lax.psum((weight_term, bias_term), "dom")
    message_blocks = messages.reshape(row_blocks, tile_size, feat_width)
    picked_messages = jnp.einsum("bs,bif->sif", row_select, message_blocks, precision=highest)
    returned = jnp.einsum("sji,sjf->sif", values, picked_messages, precision=highest)
    block_count = node_rows * lax.axis_size("dom") // tile_size
    offsets = col_ids[None, :]
    select = (offsets == jnp.arange(block_count, dtype=jnp.int32)[:, None]).astype(jnp.float32)
    source_part = lax.psum_scatter(
        jnp.einsum("ns,sif->nif", select, returned, precision=highest).reshape(
            node_rows * lax.axis_size("dom"), feat_width
        ),
        "dom",
        scatter_dimension=0,
        tiled=True,
    )
    grad_features = lax.psum(source_part, "rep")
    return (activations, grad_features, grad_weight, grad_bias)


def solution(mesh):
    return jax.shard_map(
        body,
        mesh=mesh,
        in_specs=(
            P("dom", None),
            P("dom", "rep", None, None),
            P("dom", "rep"),
            P("dom", "rep"),
            P(),
            P(),
            P("dom", None),
        ),
        out_specs=(P("dom", None), P("dom", None), P(), P()),
        check_vma=False,
    )
```

profile of v0, /device:TPU:0, one launch (start us, length us, event | category | flops | bytes accessed | tf_op | source)
XLA Modules:
  0.0 246.7 jit_solution(1948898299063535947)
XLA Ops:
  7.2 0.0 copy-start
  7.2 0.0 all-gather.2.cloned.1.call-start
  7.2 0.7 all-gather.2.cloned.1.call-update
  7.9 0.0 all-reduce.4.cloned.1.call-start
  8.0 32.6 %all-gather.2.cloned.1.call-done = f32[2048,256]{1,0:T(8,128)} async-done(((f32[256,256]{1,0:T(8,128)}), f32[2048,256]{1,0:T(8,128)}) %all-gather.2.cloned.1.call-update) | async-done | bytes 2097168 | tf_op jit(solution)/shard_map/all_gather | solution.py:16
  40.5 3.9 %fusion.8 = f32[16,128,256]{2,0,1:T(8,128)S(1)} fusion(f32[16,128,256]{2,1,0:T(8,128)} %bitcast.35, s32[16]{0:T(128)} %bitcast.40), kind=kOutput, calls=%fused_computation.8 | convolution fusion | flops 100663552 | bytes 4194368 | tf_op jit(solution)/shard_map/sn,nif->sif/dot_general | solution.py:21
  44.5 0.0 copy-done
  44.5 4.1 %fusion.6 = f32[16,256,128]{2,1,0:T(8,128)} fusion(f32[16,128,256]{2,0,1:T(8,128)S(1)} %fusion.8, bf16[1,16,128,128]{3,2,1,0:T(8,128)(2,1)S(1)} %copy-done), kind=kOutput, calls=%fused_computation.6 | convolution fusion | flops 805306368 | bytes 4718592 | tf_op jit(solution)/shard_map/sij,sjf->sif/dot_general | solution.py:22
  48.5 0.0 copy-start.3
  48.5 2.2 copy.15
  50.8 0.0 copy-start.1
  50.8 0.0 copy-start.5
  50.8 0.0 copy-start.6
  50.8 0.0 copy-done.3
  50.8 0.8 fusion.2
  51.6 0.7 copy.11
  52.4 0.0 all-reduce.4.cloned.1.call-update
  52.4 0.2 reduce-scatter.2.cloned.1.call-start
  52.6 35.2 %all-reduce.4.cloned.1.call-done = f32[256,256]{1,0:T(8,128)} async-done(((f32[256,256]{1,0:T(8,128)}), f32[256,256]{1,0:T(8,128)}) %all-reduce.4.cloned.1.call-update) | async-done | bytes 262160 | tf_op jit(solution)/shard_map/psum | solution.py:29
  87.9 0.0 copy-done.1
  87.9 0.0 copy-done.5
  87.9 0.0 copy-done.6
  87.9 2.1 fusion.25
  90.0 0.4 fusion.26
  90.4 1.1 fusion.12
  91.5 2.7 %fusion.4 = f32[16,256,128]{2,1,0:T(8,128)S(1)} fusion(f32[16,128,256]{2,0,1:T(8,128)S(1)} %fusion.12, bf16[1,16,128,128]{3,2,1,0:T(8,128)(2,1)S(1)} %copy-done), kind=kOutput, calls=%fused_computation.4 | convolution fusion | flops 805306368 | bytes 4718592 | tf_op jit(solution)/shard_map/sji,sjf->sif/dot_general | solution.py:45
  94.3 0.0 copy-start.4
  94.3 2.1 copy.18
  96.4 0.0 copy-done.4
  96.4 2.7 %fusion = f32[16,128,256]{2,0,1:T(8,128)S(1)} fusion(f32[16,256,128]{1,0,2:T(8,128)} %copy.18, s32[16]{0:T(128)S(1)} %bitcast.41), kind=kOutput, calls=%fused_computation | convolution fusion | flops 100663552 | bytes 4194368 | tf_op jit(solution)/shard_map/ns,sif->nif/dot_general | solution.py:50
  99.1 2.6 %copy.12 = f32[16,128,256]{2,1,0:T(8,128)} copy(f32[16,128,256]{2,0,1:T(8,128)S(1)} %fusion) | data formatting | bytes 4194304 | tf_op jit(solution)/shard_map/ns,sif->nif/dot_general | solution.py:50
  101.6 0.0 copy-start.2
  101.6 0.0 reduce-scatter.2.cloned.1.call-update
  101.6 0.0 all-reduce.8.cloned.1.call-start
  101.7 0.9 copy-done.2
  102.6 1.3 fusion.27
  103.9 0.0 all-reduce.8.cloned.1.call-update
  103.9 0.0 all-reduce.6.cloned.1.call-start
  103.9 38.8 %reduce-scatter.2.cloned.1.call-done = f32[256,256]{1,0:T(8,128)} async-done(((f32[2048,256]{1,0:T(8,128)}), f32[256,256]{1,0:T(8,128)}) %reduce-scatter.2.cloned.1.call-update) | async-done | bytes 262160 | tf_op jit(solution)/shard_map/reduce_scatter | solution.py:49
  142.8 0.0 all-reduce.6.cloned.1.call-update
  142.8 13.2 %psum.31 = f32[256]{0:T(256)} all-reduce(f32[256]{0:T(256)S(1)} %get-tuple-element.4), channel_id=1, replica_groups=mesh['dom'=8,'rep'=4] {'dom'}, use_global_device_ids=true, to_apply=%region_5.0 | all-reduce | flops 256 | bytes 2048 | tf_op jit(solution)/shard_map/psum | solution.py:42
  156.0 43.8 %all-reduce.8.cloned.1.call-done = f32[256,256]{1,0:T(8,128)} async-done(((f32[256,256]{1,0:T(8,128)}), f32[256,256]{1,0:T(8,128)}) %all-reduce.8.cloned.1.call-update) | async-done | bytes 262160 | tf_op jit(solution)/shard_map/psum | solution.py:42
  199.8 37.0 %all-reduce.6.cloned.1.call-done = f32[256,256]{1,0:T(8,128)} async-done(((f32[256,256]{1,0:T(8,128)}), f32[256,256]{1,0:T(8,128)}) %all-reduce.6.cloned.1.call-update) | async-done | bytes 262160 | tf_op jit(solution)/shard_map/psum | solution.py:57
  236.8 1.7 copy.30
  238.5 1.7 copy.31
Async XLA Ops:
  7.2 37.3 %copy-start = (bf16[1,16,128,128]{3,2,1,0:T(8,128)(2,1)S(1)}, bf16[1,16,128,128]{3,2,1,0:T(8,128)(2,1)}, u32[]{:S(2)}) copy-start(bf16[1,16,128,128]{3,2,1,0:T(8,128)(2,1)} %param.8) | copy-start | bytes 1572868
  7.2 33.4 %all-gather.2.cloned.1.call-start = ((), (), s32[]{:S(2)}) async-start(), calls=%async_computation.1 | async-start | bytes 2359296 | tf_op jit(solution)/shard_map/all_gather | solution.py:16
  7.9 79.9 %all-reduce.4.cloned.1.call-start = ((), (), s32[]{:S(2)}) async-start(), calls=%async_computation.2 | async-start | bytes 524288 | tf_op jit(solution)/shard_map/psum | solution.py:29
  48.5 2.3 copy-start.3
  50.8 37.1 %copy-start.1 = (f32[256,256]{1,0:T(8,128)S(1)}, f32[256,256]{1,0:T(8,128)}, u32[]{:S(2)}) copy-start(f32[256,256]{1,0:T(8,128)} %param.11) | copy-start | bytes 786436
  50.8 37.0 %copy-start.5 = (f32[256,256]{1,0:T(8,128)S(1)}, f32[256,256]{1,0:T(8,128)}, u32[]{:S(2)}) copy-start(f32[256,256]{1,0:T(8,128)} %param.13) | copy-start | bytes 786436
  50.8 37.0 %copy-start.6 = (f32[256]{0:T(256)S(1)}, f32[256]{0:T(256)}, u32[]{:S(2)}) copy-start(f32[256]{0:T(256)} %param.12) | copy-start | bytes 3076
  52.4 90.4 %reduce-scatter.2.cloned.1.call-start = ((), (), s32[]{:S(2)}) async-start(), calls=%async_computation.3 | async-start | bytes 2359296 | tf_op jit(solution)/shard_map/reduce_scatter | solution.py:49
  94.3 2.1 copy-start.4
  101.6 0.9 copy-start.2
  101.6 98.2 %all-reduce.8.cloned.1.call-start = ((), (), s32[]{:S(2)}) async-start(), calls=%async_computation.5 | async-start | bytes 524288 | tf_op jit(solution)/shard_map/psum | solution.py:42
  103.9 132.9 %all-reduce.6.cloned.1.call-start = ((), (), s32[]{:S(2)}) async-start(), calls=%async_computation.4 | async-start | bytes 524288 | tf_op jit(solution)/shard_map/psum | solution.py:57
Sparse Core Ops, SparseCore 0:
  9.9 30.5 all-gather.1
  52.5 35.2 all-reduce.3
  101.8 40.9 reduce-scatter.1
  146.2 53.5 all-reduce.7
  202.1 34.6 all-reduce.5
where the time goes:
time: 247 us
  waiting for transfers between devices  188 us (76%)
  matrix products  19.2 us (8%)
  between operations  13.9 us (6%)
  blocking collectives  13.2 us (5%)
  local copies, waits for them, and re-layouts  11.8 us (5%)
    psum x1, waiting for transfers between devices, body(): grad_weight, grad_bias = lax.psum((weight_term, bias_term), 'dom')  43.8 us
    reduce_scatter x1, waiting for transfers between devices, body(): lax.psum_scatter(jnp.einsum('ns,sif->nif', select, returned, precision=hi...  38.8 us
    psum x1, waiting for transfers between devices, body(): grad_features = lax.psum(source_part, 'rep')  37 us
    psum x1, waiting for transfers between devices, body(): aggregated = lax.psum(partial_rows, 'rep')  35.2 us
    all_gather x1, waiting for transfers between devices, body(): shard_piece = lax.all_gather(features, 'dom', axis=0, tiled=True)  32.6 us
    psum x1, blocking collectives, body(): grad_weight, grad_bias = lax.psum((weight_term, bias_term), 'dom')  13.2 us
  transfers between devices with their start and end apart: 5, of which 5 were waited for; matrix products, arithmetic and copies ran while one was open for 1% of the time, Pallas kernels for 0%

commit v1 on v0

--- a/solution.py
+++ b/solution.py
@@ -2,6 +2,12 @@
 import jax.numpy as jnp
 from jax import lax
 from jax.sharding import PartitionSpec as P
+
+
+def gather_and_add(x, name):
+    terms = lax.all_gather(x, name, axis=0, tiled=False)
+    total = terms.sum(axis=0)
+    return total
 
 
 def body(features, tile_values, tile_rows, tile_cols, weight, bias, cotangent):
@@ -54,7 +60,7 @@
         scatter_dimension=0,
         tiled=True,
     )
-    grad_features = lax.psum(source_part, "rep")
+    grad_features = gather_and_add(source_part, "rep")
     return (activations, grad_features, grad_weight, grad_bias)
 
 

time: 247 us -> 237 us (0.960)
  waiting for transfers between devices: 188 us -> 179 us
  local copies, waits for them, and re-layouts: 11.8 us -> 9.3 us
    psum x1 -> x0, waiting for transfers between devices: 37 us -> none  [body(): grad_features = lax.psum(source_part, 'rep')]
    all_gather x0 -> x1, waiting for transfers between devices: none -> 14.7 us  [gather_and_add(): terms = lax.all_gather(x, name, axis=0, tiled=False)]
    psum x1, waiting for transfers between devices: 43.8 us -> 54.5 us  [body(): grad_weight, grad_bias = lax.psum((weight_term, bias_term), 'dom')]
    unnamed x16 -> x15, local copies, waits for them, and re-layouts: 4.25 us -> 1.71 us
where the time goes in v1:
time: 237 us
  waiting for transfers between devices  179 us (76%)
  matrix products  19.2 us (8%)
  between operations  13.9 us (6%)
  blocking collectives  13.2 us (6%)
  local copies, waits for them, and re-layouts  9.3 us (4%)
    psum x1, waiting for transfers between devices, body(): grad_weight, grad_bias = lax.psum((weight_term, bias_term), 'dom')  54.5 us
    reduce_scatter x1, waiting for transfers between devices, body(): lax.psum_scatter(jnp.einsum('ns,sif->nif', select, returned, precision=hi...  41.1 us
    psum x1, waiting for transfers between devices, body(): aggregated = lax.psum(partial_rows, 'rep')  35.2 us
    all_gather x1, waiting for transfers between devices, body(): shard_piece = lax.all_gather(features, 'dom', axis=0, tiled=True)  32.6 us
    all_gather x1, waiting for transfers between devices, gather_and_add(): terms = lax.all_gather(x, name, axis=0, tiled=False)  14.7 us
    psum x1, blocking collectives, body(): grad_weight, grad_bias = lax.psum((weight_term, bias_term), 'dom')  13.2 us
  transfers between devices with their start and end apart: 5, of which 5 were waited for; matrix products, arithmetic and copies ran while one was open for 1% of the time, Pallas kernels for 0%

profile of v1, /device:TPU:0, one launch (start us, length us, event | category | flops | bytes accessed | tf_op | source)
XLA Modules:
  0.0 236.9 jit_solution(10176714849986037155)
XLA Ops:
  7.2 0.0 copy-start
  7.2 0.0 all-gather.4.cloned.1.call-start
  7.2 0.7 all-gather.4.cloned.1.call-update
  7.9 0.0 all-reduce.3.cloned.1.call-start
  8.0 32.6 %all-gather.4.cloned.1.call-done = f32[2048,256]{1,0:T(8,128)} async-done(((f32[256,256]{1,0:T(8,128)}), f32[2048,256]{1,0:T(8,128)}) %all-gather.4.cloned.1.call-update) | async-done | bytes 2097168 | tf_op jit(solution)/shard_map/all_gather | solution.py:22
  40.5 3.9 %fusion.8 = f32[16,128,256]{2,0,1:T(8,128)S(1)} fusion(f32[16,128,256]{2,1,0:T(8,128)} %bitcast.36, s32[16]{0:T(128)} %bitcast.42), kind=kOutput, calls=%fused_computation.8 | convolution fusion | flops 100663552 | bytes 4194368 | tf_op jit(solution)/shard_map/sn,nif->sif/dot_general | solution.py:27
  44.5 0.0 copy-done
  44.5 4.1 %fusion.6 = f32[16,256,128]{2,1,0:T(8,128)} fusion(f32[16,128,256]{2,0,1:T(8,128)S(1)} %fusion.8, bf16[1,16,128,128]{3,2,1,0:T(8,128)(2,1)S(1)} %copy-done), kind=kOutput, calls=%fused_computation.6 | convolution fusion | flops 805306368 | bytes 4718592 | tf_op jit(solution)/shard_map/sij,sjf->sif/dot_general | solution.py:28
  48.5 0.0 copy-start.3
  48.5 2.2 copy.15
  50.8 0.0 copy-start.1
  50.8 0.0 copy-start.5
  50.8 0.0 copy-start.6
  50.8 0.0 copy-done.3
  50.8 0.8 fusion.2
  51.6 0.7 copy.11
  52.4 0.0 all-reduce.3.cloned.1.call-update
  52.4 0.2 reduce-scatter.2.cloned.1.call-start
  52.6 35.2 %all-reduce.3.cloned.1.call-done = f32[256,256]{1,0:T(8,128)} async-done(((f32[256,256]{1,0:T(8,128)}), f32[256,256]{1,0:T(8,128)}) %all-reduce.3.cloned.1.call-update) | async-done | bytes 262160 | tf_op jit(solution)/shard_map/psum | solution.py:35
  87.9 0.0 copy-done.1
  87.9 0.0 copy-done.5
  87.9 0.0 copy-done.6
  87.9 2.1 fusion.25
  90.0 0.4 fusion.26
  90.4 1.1 fusion.12
  91.5 2.7 %fusion.4 = f32[16,256,128]{2,1,0:T(8,128)S(1)} fusion(f32[16,128,256]{2,0,1:T(8,128)S(1)} %fusion.12, bf16[1,16,128,128]{3,2,1,0:T(8,128)(2,1)S(1)} %copy-done), kind=kOutput, calls=%fused_computation.4 | convolution fusion | flops 805306368 | bytes 4718592 | tf_op jit(solution)/shard_map/sji,sjf->sif/dot_general | solution.py:51
  94.3 0.0 copy-start.4
  94.3 2.1 copy.18
  96.4 0.0 copy-done.4
  96.4 2.7 %fusion = f32[16,128,256]{2,0,1:T(8,128)S(1)} fusion(f32[16,256,128]{1,0,2:T(8,128)} %copy.18, s32[16]{0:T(128)S(1)} %bitcast.43), kind=kOutput, calls=%fused_computation | convolution fusion | flops 100663552 | bytes 4194368 | tf_op jit(solution)/shard_map/ns,sif->nif/dot_general | solution.py:56
  99.1 2.6 %copy.12 = f32[16,128,256]{2,1,0:T(8,128)} copy(f32[16,128,256]{2,0,1:T(8,128)S(1)} %fusion) | data formatting | bytes 4194304 | tf_op jit(solution)/shard_map/ns,sif->nif/dot_general | solution.py:56
  101.6 0.0 copy-start.2
  101.6 0.0 reduce-scatter.2.cloned.1.call-update
  101.6 0.0 all-gather.6.cloned.1.call-start
  101.7 41.1 %reduce-scatter.2.cloned.1.call-done = f32[256,256]{1,0:T(8,128)} async-done(((f32[2048,256]{1,0:T(8,128)}), f32[256,256]{1,0:T(8,128)}) %reduce-scatter.2.cloned.1.call-update) | async-done | bytes 262160 | tf_op jit(solution)/shard_map/reduce_scatter | solution.py:55
  142.8 0.0 all-gather.6.cloned.1.call-update
  142.8 0.0 all-reduce.5.cloned.1.call-start
  142.8 0.0 copy-done.2
  142.8 1.3 fusion.27
  144.1 0.0 all-reduce.5.cloned.1.call-update
  144.2 13.2 %psum.23 = f32[256]{0:T(256)} all-reduce(f32[256]{0:T(256)S(1)} %get-tuple-element.4), channel_id=1, replica_groups=mesh['dom'=8,'rep'=4] {'dom'}, use_global_device_ids=true, to_apply=%region_5.0 | all-reduce | flops 256 | bytes 2048 | tf_op jit(solution)/shard_map/psum | solution.py:48
  157.4 14.7 %all-gather.6.cloned.1.call-done = f32[1024,256]{1,0:T(8,128)} async-done(((f32[256,256]{1,0:T(8,128)}), f32[1024,256]{1,0:T(8,128)}) %all-gather.6.cloned.1.call-update) | async-done | bytes 1048592 | tf_op jit(solution)/shard_map/all_gather | solution.py:8
  172.1 2.0 reduce_sum.18
  174.2 54.5 %all-reduce.5.cloned.1.call-done = f32[256,256]{1,0:T(8,128)} async-done(((f32[256,256]{1,0:T(8,128)}), f32[256,256]{1,0:T(8,128)}) %all-reduce.5.cloned.1.call-update) | async-done | bytes 262160 | tf_op jit(solution)/shard_map/psum | solution.py:48
  228.7 1.7 copy.29
Async XLA Ops:
  7.2 37.3 %copy-start = (bf16[1,16,128,128]{3,2,1,0:T(8,128)(2,1)S(1)}, bf16[1,16,128,128]{3,2,1,0:T(8,128)(2,1)}, u32[]{:S(2)}) copy-start(bf16[1,16,128,128]{3,2,1,0:T(8,128)(2,1)} %param.8) | copy-start | bytes 1572868
  7.2 33.4 %all-gather.4.cloned.1.call-start = ((), (), s32[]{:S(2)}) async-start(), calls=%async_computation.1 | async-start | bytes 2359296 | tf_op jit(solution)/shard_map/all_gather | solution.py:22
  7.9 79.9 %all-reduce.3.cloned.1.call-start = ((), (), s32[]{:S(2)}) async-start(), calls=%async_computation.2 | async-start | bytes 524288 | tf_op jit(solution)/shard_map/psum | solution.py:35
  48.5 2.3 copy-start.3
  50.8 37.1 %copy-start.1 = (f32[256,256]{1,0:T(8,128)S(1)}, f32[256,256]{1,0:T(8,128)}, u32[]{:S(2)}) copy-start(f32[256,256]{1,0:T(8,128)} %param.11) | copy-start | bytes 786436
  50.8 37.0 %copy-start.5 = (f32[256,256]{1,0:T(8,128)S(1)}, f32[256,256]{1,0:T(8,128)}, u32[]{:S(2)}) copy-start(f32[256,256]{1,0:T(8,128)} %param.13) | copy-start | bytes 786436
  50.8 37.0 %copy-start.6 = (f32[256]{0:T(256)S(1)}, f32[256]{0:T(256)}, u32[]{:S(2)}) copy-start(f32[256]{0:T(256)} %param.12) | copy-start | bytes 3076
  52.4 90.4 %reduce-scatter.2.cloned.1.call-start = ((), (), s32[]{:S(2)}) async-start(), calls=%async_computation.3 | async-start | bytes 2359296 | tf_op jit(solution)/shard_map/reduce_scatter | solution.py:55
  94.3 2.1 copy-start.4
  101.6 41.2 %copy-start.2 = (f32[256,256]{1,0:T(8,128)S(1)}, f32[256,256]{1,0:T(8,128)}, u32[]{:S(2)}) copy-start(f32[256,256]{1,0:T(8,128)} %all-reduce.3.cloned.1.call-done) | copy-start | bytes 786436
  101.6 70.5 %all-gather.6.cloned.1.call-start = ((), (), s32[]{:S(2)}) async-start(), calls=%async_computation.5 | async-start | bytes 1310720 | tf_op jit(solution)/shard_map/all_gather | solution.py:8
  142.8 85.9 %all-reduce.5.cloned.1.call-start = ((), (), s32[]{:S(2)}) async-start(), calls=%async_computation.4 | async-start | bytes 524288 | tf_op jit(solution)/shard_map/psum | solution.py:48
Sparse Core Ops, SparseCore 0:
  9.9 30.5 all-gather.3
  52.5 35.2 all-reduce.2
  101.8 40.9 reduce-scatter.1
  144.2 27.9 all-gather.5
  175.6 53.0 all-reduce.4
